TPU v7x, 32 devices: a whole 2x2x4 slice. The times are simulated.
32 devices in a mesh: row: 2 (over x), col: 16 (over z, y, core).
Axes of the slice: x: 2, y: 2, z: 4, core: 2. Of those that a mesh axis runs over, the one named last changes fastest.
Arguments:
- blocks: bfloat16 [2, 16, 8, 512, 512], P('row', 'col'), may hold values from -0.046875 to 0.046875
- block_rows: int32 [2, 16, 8], P('row', 'col'), may hold values from 0 to 3, as said below
- block_cols: int32 [2, 16, 8], P('row', 'col'), may hold values from 0 to 3
- sketch: bfloat16 [4096, 32], P('row'), may hold values from -6 to 6
- theta: float32 [32768], P('col'), may hold values from 0.1 to 10
- rhs: float32 [4096], P('row'), may hold values from -6 to 6
Outputs:
- solution: float32 [4096], P(('row', 'col'))
- residual: float32 [4096], P(('row', 'col'))
- precond_residual: float32 [4096], P(('row', 'col'))
Inputs may be any that keep to these rules, and one draw needn't show every extreme that they name: Within one tile the pairs (block_rows, block_cols) are all different.
All inputs are finite; a program needn't handle non-finite values.
Results may differ from a plain program's by a relative error of at most 0.005.
Values may be sent and summed in bfloat16 or wider, within the bound.
A program may use at most 64 MiB of HBM per device.

v0:
```python
import jax
import jax.numpy as jnp
from jax import lax
from jax.sharding import PartitionSpec as P

precond_shift = 1.0
regularize = 0.5


def tile_transpose(values, rows_idx, cols_idx, inputs, col_count):
    order = values.shape[1]
    width = inputs.shape[1]
    picked = inputs.reshape(-1, order, width)[rows_idx]
    product = jnp.einsum("nab,nak->nbk", values, picked, preferred_element_type=jnp.float32)
    onehot = (cols_idx[:, None] == jnp.arange(col_count, dtype=jnp.int32)[None, :]).astype(
        jnp.float32
    )
    merged = jnp.einsum("nj,nbk->jbk", onehot, product, precision=lax.Precision.HIGHEST)
    return merged.reshape(col_count * order, width)


def tile_forward(values, rows_idx, cols_idx, inputs, row_count):
    order = values.shape[1]
    width = inputs.shape[1]
    picked = inputs.reshape(-1, order, width)[cols_idx]
    product = jnp.einsum("nab,nbk->nak", values, picked, preferred_element_type=jnp.float32)
    onehot = (rows_idx[:, None] == jnp.arange(row_count, dtype=jnp.int32)[None, :]).astype(
        jnp.float32
    )
    merged = jnp.einsum("ni,nak->iak", onehot, product, precision=lax.Precision.HIGHEST)
    return merged.reshape(row_count * order, width)


def solve_gram(factor, vector):
    middle = lax.linalg.triangular_solve(factor, vector[:, None], left_side=True, lower=True)
    result = lax.linalg.triangular_solve(
        factor, middle, left_side=True, lower=True, transpose_a=True
    )
    return result[:, 0]


def shards(blocks, block_rows, block_cols, sketch, theta, rhs):
    values = blocks[0, 0]
    rows_idx = block_rows[0, 0]
    cols_idx = block_cols[0, 0]
    order = values.shape[1]
    local_rows = sketch.shape[0]
    row_count = local_rows // order
    col_count = theta.shape[0] // order
    share = local_rows // lax.axis_size("col")
    offset = lax.axis_index("col") * share
    sketch_f = sketch.astype(jnp.float32)
    sketch_part = lax.dynamic_slice_in_dim(sketch_f, offset, share, 0)
    rhs_part = lax.dynamic_slice_in_dim(rhs, offset, share, 0)
    col_terms = tile_transpose(values, rows_idx, cols_idx, sketch, col_count)
    sketch_cols = lax.psum(col_terms, "row")
    scaled = (theta[:, None] * sketch_cols).astype(jnp.bfloat16)
    row_terms = tile_forward(values, rows_idx, cols_idx, scaled, row_count)
    ysketch = lax.psum(row_terms, "col") + regularize * sketch_f
    y_part = lax.dynamic_slice_in_dim(ysketch, offset, share, 0)
    cross = jnp.dot(sketch_part.T, y_part, precision=lax.Precision.HIGHEST)
    gram_terms = precond_shift * 0.5 * (cross + cross.T) + jnp.dot(
        y_part.T, y_part, precision=lax.Precision.HIGHEST
    )
    yb_terms = jnp.dot(rhs_part, y_part, precision=lax.Precision.HIGHEST)
    gram, sketched_rhs = lax.psum((gram_terms, yb_terms), ("row", "col"))
    factor = jnp.linalg.cholesky(gram)
    coeffs = solve_gram(factor, sketched_rhs)
    direction_full = (
        rhs - jnp.dot(ysketch, coeffs, precision=lax.Precision.HIGHEST)
    ) / precond_shift
    direction = lax.dynamic_slice_in_dim(direction_full, offset, share, 0)
    dir_low = direction_full.astype(jnp.bfloat16)
    image_terms = tile_transpose(values, rows_idx, cols_idx, dir_low[:, None], col_count)[:, 0]
    image_cols = lax.psum(image_terms, "row")
    image_scaled = (theta * image_cols).astype(jnp.bfloat16)
    product_terms = tile_forward(values, rows_idx, cols_idx, image_scaled[:, None], row_count)[:, 0]
    image_full = lax.psum(product_terms, "col")
    image = lax.dynamic_slice_in_dim(image_full, offset, share, 0) + regularize * direction
    along = lax.psum(jnp.sum(rhs_part * direction), ("row", "col"))
    curvature = lax.psum(jnp.sum(direction * image), ("row", "col"))
    alpha = along / curvature
    residual = rhs_part - alpha * image
    sketched_res = lax.psum(
        jnp.dot(residual, y_part, precision=lax.Precision.HIGHEST), ("row", "col")
    )
    solution = alpha * direction
    res_coeffs = solve_gram(factor, sketched_res)
    precond_residual = (
        residual - jnp.dot(y_part, res_coeffs, precision=lax.Precision.HIGHEST)
    ) / precond_shift
    return (solution, residual, precond_residual)


def solution(mesh):
    in_specs = (
        P("row", "col", None, None, None),
        P("row", "col", None),
        P("row", "col", None),
        P("row", None),
        P("col"),
        P("row"),
    )
    out_specs = (P(("row", "col")), P(("row", "col")), P(("row", "col")))
    return jax.shard_map(shards, mesh=mesh, in_specs=in_specs, out_specs=out_specs, check_vma=False)
```

profile of v0, /device:TPU:0, one launch (start us, length us, event | category | flops | bytes accessed | tf_op | source)
XLA Modules:
  0.0 318.9 jit_solution(7802863516477958516)
XLA Ops:
  7.2 0.0 copy-start.4
  7.2 0.0 all-reduce.5.cloned.1.call-start
  7.2 0.9 copy.48
  8.1 0.7 fusion.47
  8.8 0.0 copy-start.1
  8.8 0.6 gather_fusion
  9.4 3.0 fusion.8
  12.4 0.0 copy-done.4
  12.4 0.7 fusion.17
  13.1 0.0 copy-start.5
  13.1 0.8 copy.25
  13.9 0.0 all-reduce.5.cloned.1.call-update
  13.9 0.0 all-reduce.7.cloned.1.call-start
  14.0 26.0 %all-reduce.5.cloned.1.call-done = f32[2048,32]{0,1:T(8,128)} async-done(((f32[2048,32]{0,1:T(8,128)}), f32[2048,32]{0,1:T(8,128)}) %all-reduce.5.cloned.1.call-update) | async-done | bytes 262160 | tf_op jit(solution)/shard_map/psum | solution.py:56
  39.9 0.0 copy-done.1
  39.9 1.0 multiply_convert_fusion
  40.9 0.0 copy-start
  40.9 0.6 gather_fusion.1
  41.5 0.0 copy-start.2
  41.5 3.5 %fusion.11 = f32[8,512,32]{1,2,0:T(8,128)S(1)} fusion(bf16[8,512,32]{1,2,0:T(8,128)(2,1)S(1)} %gather_fusion.1, bf16[1,1,8,512,512]{4,3,2,1,0:T(8,128)(2,1)} %param.10), kind=kOutput, calls=%fused_computation.13 | convolution fusion | flops 134217728 | bytes 4980736 | tf_op jit(solution)/shard_map/nab,nbk->nak/dot_general | solution.py:26
  45.0 0.0 copy-done.5
  45.0 0.7 fusion.15
  45.7 0.8 copy.26
  46.5 0.0 all-reduce.7.cloned.1.call-update
  46.5 88.9 %all-reduce.7.cloned.1.call-done = f32[2048,32]{0,1:T(8,128)} async-done(((f32[2048,32]{0,1:T(8,128)}), f32[2048,32]{0,1:T(8,128)}) %all-reduce.7.cloned.1.call-update) | async-done | bytes 262160 | tf_op jit(solution)/shard_map/psum | solution.py:59
  135.4 0.0 copy-done
  135.4 1.0 multiply_add_fusion
  136.4 0.1 fusion.36
  136.5 0.1 copy.17
  136.6 0.2 convolution_add_fusion
  136.8 0.0 copy-done.2
  136.8 0.2 convolution_bitcast_fusion.8
  137.0 40.9 %all-reduce.1 = (f32[32,1]{0,1:T(1,128)S(1)}, f32[32,32]{1,0:T(8,128)S(1)}) all-reduce(f32[32,1]{0,1:T(1,128)S(1)} %convolution_bitcast_fusion.8, f32[32,32]{1,0:T(8,128)S(1)} %convolution_add_fusion), channel_id=1, replica_groups=mesh['row'=2,'col'=16] {'row','col'}, use_global_device_ids=true, to_apply=%region_5.6 | all-reduce | flops 1056 | bytes 8448 | tf_op jit(solution)/shard_map/psum | solution.py:66
  177.9 0.1 copy.18
  178.0 2.9 cholesky.18
  180.9 0.6 compare_reduce_fusion
  181.6 0.7 fusion.19
  182.2 2.4 custom-call.12
  184.6 0.2 convolution_bitcast_fusion.7
  184.8 0.1 convolution_bitcast_fusion.6
  184.9 0.3 fusion.58
  185.3 0.6 gather_fusion.2
  185.8 2.8 fusion.2
  188.7 0.1 convolution_bitcast_fusion.1
  188.8 5.2 %psum.68 = f32[2048]{0:T(1024)S(1)} all-reduce(f32[2048]{0:T(1024)S(1)} %bitcast.149), channel_id=1, replica_groups=mesh['row'=2,'col'=16] {'row'}, use_global_device_ids=true, to_apply=%region_8.11 | all-reduce | flops 2048 | bytes 16384 | tf_op jit(solution)/shard_map/psum | solution.py:75
  194.1 0.6 gather_fusion.3
  194.6 3.4 %fusion = f32[8,1,512]{2,1,0:T(1,128)S(1)} fusion(bf16[1,1,8,512,512]{4,3,2,1,0:T(8,128)(2,1)} %param.10, bf16[8,512,1]{1,0,2:T(8,128)(2,1)S(1)} %bitcast.147), kind=kOutput, calls=%fused_computation.4 | convolution fusion | flops 4194304 | bytes 4218880 | tf_op jit(solution)/shard_map/nab,nbk->nak/dot_general | solution.py:26
  198.0 0.1 convolution_bitcast_fusion
  198.2 30.4 %psum.69 = f32[2048]{0:T(1024)S(1)} all-reduce(f32[2048]{0:T(1024)S(1)} %bitcast.150), channel_id=1, replica_groups=mesh['row'=2,'col'=16] {'col'}, use_global_device_ids=true, to_apply=%region_9.12 | all-reduce | flops 2048 | bytes 16384 | tf_op jit(solution)/shard_map/psum | solution.py:78
  228.6 0.7 multiply_reduce_fusion
  229.3 37.2 %all-reduce = (f32[]{:T(128)}, f32[]{:T(128)}) all-reduce(f32[]{:T(128)} %get-tuple-element.6, f32[]{:T(128)} %get-tuple-element.5), channel_id=1, replica_groups=mesh['row'=2,'col'=16] {'row','col'}, use_global_device_ids=true, to_apply=%region_7.10 | all-reduce | flops 2 | bytes 16 | tf_op jit(solution)/shard_map/psum | solution.py:80
  267.8 0.6 multiply_subtract_fusion
  268.4 0.0 copy-start.3
  268.4 0.1 convolution_bitcast_fusion.5
  268.5 42.5 %psum.71 = f32[32,1]{0,1:T(1,128)S(1)} all-reduce(f32[32,1]{0,1:T(1,128)S(1)} %convolution_bitcast_fusion.5), channel_id=1, replica_groups=mesh['row'=2,'col'=16] {'row','col'}, use_global_device_ids=true, to_apply=%region_12.15 | all-reduce | flops 32 | bytes 256 | tf_op jit(solution)/shard_map/psum | solution.py:84
  311.1 0.1 convolution_bitcast_fusion.4
  311.2 0.1 convolution_bitcast_fusion.3
  311.3 0.7 fusion.14
  312.0 0.0 copy-done.3
  (12 shorter events, 0.1 us)
Async XLA Ops:
  7.2 5.2 %copy-start.4 = (s32[1,1,8]{2,1,0:T(1,128)S(1)}, s32[1,1,8]{2,1,0:T(1,128)}, u32[]{:S(2)}) copy-start(s32[1,1,8]{2,1,0:T(1,128)} %param.12) | copy-start | bytes 100
  7.2 32.7 %all-reduce.5.cloned.1.call-start = ((), (), s32[]{:S(2)}) async-start(), calls=%async_computation | async-start | bytes 524288 | tf_op jit(solution)/shard_map/psum | solution.py:56
  8.8 31.1 %copy-start.1 = (f32[2048]{0:T(1024)S(1)}, f32[2048]{0:T(1024)}, u32[]{:S(2)}) copy-start(f32[2048]{0:T(1024)} %param.14) | copy-start | bytes 24580
  13.1 31.9 %copy-start.5 = (s32[1,1,8]{2,1,0:T(1,128)S(1)}, s32[1,1,8]{2,1,0:T(1,128)}, u32[]{:S(2)}) copy-start(s32[1,1,8]{2,1,0:T(1,128)} %param.11) | copy-start | bytes 100
  13.9 121.5 %all-reduce.7.cloned.1.call-start = ((), (), s32[]{:S(2)}) async-start(), calls=%async_computation.1 | async-start | bytes 524288 | tf_op jit(solution)/shard_map/psum | solution.py:59
  40.9 94.5 %copy-start = (bf16[2048,32]{0,1:T(8,128)(2,1)S(1)}, bf16[2048,32]{0,1:T(8,128)(2,1)}, u32[]{:S(2)}) copy-start(bf16[2048,32]{0,1:T(8,128)(2,1)} %param.13) | copy-start | bytes 393220
  41.5 95.3 %copy-start.2 = (f32[2048]{0:T(1024)S(1)}, f32[2048]{0:T(1024)}, u32[]{:S(2)}) copy-start(f32[2048]{0:T(1024)} %param.15) | copy-start | bytes 24580
  268.4 43.6 %copy-start.3 = (f32[128]{0:T(128)}, f32[128]{0:T(128)S(1)}, u32[]{:S(2)}) copy-start(f32[128]{0:T(128)S(1)} %get-tuple-element.13) | copy-start | bytes 1540
Sparse Core Ops, SparseCore 0:
  14.0 25.8 all-reduce.4
  46.6 88.7 all-reduce.6
where the time goes:
time: 320 us; the launch traced here: 319 us
  blocking collectives  156 us (49%)
  waiting for transfers between devices  115 us (36%)
  matrix products  16.5 us (5%)
  between operations  15.6 us (5%)
  other arithmetic  10.6 us (3%)
  local copies, waits for them, and re-layouts  4.98 us (2%)
    psum x1, waiting for transfers between devices, shards(): ysketch = lax.psum(row_terms, 'col') + regularize * sketch_f  88.9 us
    psum x1, blocking collectives, shards(): lax.psum(jnp.dot(residual, y_part, precision=lax.Precision.HIGHEST), ('ro...  42.5 us
    psum x1, blocking collectives, shards(): gram, sketched_rhs = lax.psum((gram_terms, yb_terms), ('row', 'col'))  40.9 us
    psum x1, blocking collectives, shards(): along = lax.psum(jnp.sum(rhs_part * direction), ('row', 'col'))  37.2 us
    psum x1, blocking collectives, shards(): image_full = lax.psum(product_terms, 'col')  30.4 us
    psum x1, waiting for transfers between devices, shards(): sketch_cols = lax.psum(col_terms, 'row')  26 us
    dot_general x2, matrix products, tile_forward(): jnp.einsum('nab,nbk->nak', values, picked, preferred_element_type=jnp.flo...  6.87 us
  transfers between devices with their start and end apart: 2, of which 2 were waited for; matrix products, arithmetic and copies ran while one was open for 0% of the time, Pallas kernels for 0%

commit v1 on v0

--- a/solution.py
+++ b/solution.py
@@ -1,10 +1,314 @@
+import functools
+
 import jax
 import jax.numpy as jnp
 from jax import lax
+from jax.experimental import pallas as pl
+from jax.experimental.pallas import tpu as pltpu
 from jax.sharding import PartitionSpec as P
 
 precond_shift = 1.0
 regularize = 0.5
+MESH = pl.DeviceIdType.MESH
+HIGHEST = lax.Precision.HIGHEST
+PLANE = 4
+LANES = 128
+
+
+def dot_nt(left, right, precision=None):
+    return lax.dot_general(
+        left, right, (((1,), (1,)), ((), ())), precision=precision, preferred_element_type=jnp.float32
+    )
+
+
+def spread(source, index, place, copies, height):
+    picked = source[index]
+    width, lanes = picked.shape
+    if width == 1:
+        tall = jnp.broadcast_to(picked, (height, lanes))
+    else:
+        tall = jnp.concatenate([picked] * copies, axis=0)
+    group = lax.broadcasted_iota(jnp.int32, (height, lanes), 0) // width
+    return jnp.where(group == place, tall, 0.0).astype(jnp.bfloat16)
+
+
+def eliminate(matrix, right):
+    order = matrix.shape[0]
+    matrix = jnp.concatenate([matrix, jnp.zeros((order, LANES - order), jnp.float32)], axis=1)
+    at = lax.broadcasted_iota(jnp.int32, (order, LANES), 0)
+    for k in range(order):
+        inverse = 1.0 / matrix[k : k + 1, k : k + 1]
+        column = jnp.broadcast_to(matrix[:, k : k + 1], (order, LANES))
+        row_m = matrix[k : k + 1, :] * inverse
+        row_r = right[k : k + 1, :] * inverse
+        matrix = jnp.where(at == k, row_m, matrix - column * row_m)
+        right = jnp.where(at == k, row_r, right - column * row_r)
+    return right
+
+
+def kernel(
+    cols,
+    row_blocks,
+    col_blocks,
+    brow_ref,
+    bcol_ref,
+    blocks_ref,
+    sketch_ref,
+    theta_ref,
+    rhs_ref,
+    sol_ref,
+    res_ref,
+    pre_ref,
+    vals,
+    sk_t,
+    s_src,
+    s_dst,
+    zs,
+    y_src,
+    y_dst,
+    g_plane,
+    g_depth,
+    d_all,
+    xs,
+    e_src,
+    e_dst,
+    zv,
+    f_src,
+    f_dst,
+    h_plane,
+    h_depth,
+    block_sem,
+    pair_sem,
+    y_sem,
+    g_sem,
+    d_sem,
+    f_sem,
+    h_sem,
+):
+    me_r = lax.axis_index("row")
+    me_c = lax.axis_index("col")
+    stored, order = vals.shape[0], vals.shape[1]
+    width = sketch_ref.shape[1]
+    pieces = order // LANES
+    depth = cols // PLANE
+    z, q = me_c // PLANE, me_c % PLANE
+    plane = 2 * PLANE
+    me_p = me_r * PLANE + q
+    pending = []
+
+    loads = []
+    for n in range(stored):
+        load = pltpu.make_async_copy(blocks_ref.at[n], vals.at[n], block_sem.at[n])
+        load.start()
+        loads.append(load)
+
+    barrier = pltpu.get_barrier_semaphore()
+    for t in range(1, cols):
+        pl.semaphore_signal(
+            barrier, inc=1, device_id=(me_r, lax.rem(me_c + t, cols)), device_id_type=MESH
+        )
+    for u in range(PLANE):
+        pl.semaphore_signal(
+            barrier, inc=1, device_id=(1 - me_r, z * PLANE + u), device_id_type=MESH
+        )
+
+    def send(src, dst, sems, at, device):
+        copy = pltpu.make_async_remote_copy(
+            src_ref=src,
+            dst_ref=dst,
+            send_sem=sems.at[0, at],
+            recv_sem=sems.at[1, at],
+            device_id=device,
+            device_id_type=MESH,
+        )
+        copy.start()
+        pending.append(copy)
+        return copy
+
+    def all_reduce(value, first, second, sems):
+        first[me_p] = value
+        copies = []
+        for u in range(1, plane):
+            peer = lax.rem(me_p + u, plane)
+            device = (peer // PLANE, z * PLANE + lax.rem(peer, PLANE))
+            copies.append(send(first.at[me_p], first.at[me_p], sems, u - 1, device))
+        for copy in copies:
+            copy.wait_recv()
+        total = first[0]
+        for u in range(1, plane):
+            total = total + first[u]
+        second[z] = total
+        copies = []
+        for u in range(1, depth):
+            device = (me_r, lax.rem(z + u, depth) * PLANE + q)
+            copies.append(send(second.at[z], second.at[z], sems, plane - 2 + u, device))
+        for copy in copies:
+            copy.wait_recv()
+        total = second[0]
+        for u in range(1, depth):
+            total = total + second[u]
+        return total
+
+    def scatter_sum(src, dst, sems):
+        copies = []
+        for t in range(1, cols):
+            to = lax.rem(me_c + t, cols)
+            copies.append(send(src.at[to], dst.at[t], sems, t, (me_r, to)))
+        total = src[me_c]
+        for t, copy in enumerate(copies, 1):
+            copy.wait_recv()
+            total = total + dst[t]
+        return total
+
+    def strip(ref, j):
+        return jnp.concatenate([ref[pieces * j + p : pieces * j + p + 1, :] for p in range(pieces)], axis=1)
+
+    eye = (
+        lax.broadcasted_iota(jnp.int32, (width, width), 0)
+        == lax.broadcasted_iota(jnp.int32, (width, width), 1)
+    )
+    eye = jnp.where(eye, 1.0, 0.0).astype(jnp.bfloat16)
+    for i in range(row_blocks):
+        sk_t[i] = dot_nt(eye, sketch_ref[i * order : (i + 1) * order, :])
+    omega = dot_nt(eye, sketch_ref[pl.ds(pl.multiple_of(me_c * LANES, LANES), LANES), :])
+    rhs = jnp.broadcast_to(rhs_ref[pl.ds(me_c, 1), :], (8, LANES))
+
+    total = jnp.zeros((col_blocks * width, order), jnp.float32)
+    for n in range(stored):
+        left = spread(sk_t, brow_ref[n], bcol_ref[n], col_blocks, col_blocks * width)
+        loads[n].wait()
+        total = total + jnp.dot(left, vals[n], preferred_element_type=jnp.float32)
+    s_src[...] = total
+    pl.semaphore_wait(barrier, cols - 1 + PLANE)
+    send(s_src, s_dst, pair_sem, 0, (1 - me_r, me_c)).wait_recv()
+    for j in range(col_blocks):
+        part = slice(j * width, (j + 1) * width)
+        scaled = (strip(theta_ref, j) * (s_src[part, :] + s_dst[part, :])).astype(jnp.bfloat16)
+        zs[j] = scaled.astype(jnp.float32)
+
+    total = jnp.zeros((row_blocks * width, order), jnp.float32)
+    for n in range(stored):
+        left = spread(zs, bcol_ref[n], brow_ref[n], row_blocks, row_blocks * width)
+        total = total + dot_nt(left, vals[n])
+    for i in range(row_blocks):
+        for p in range(pieces):
+            y_src[pieces * i + p] = total[i * width : (i + 1) * width, p * LANES : (p + 1) * LANES]
+    y_t = scatter_sum(y_src, y_dst, y_sem) + regularize * omega
+
+    both = y_t + precond_shift * omega
+    first = dot_nt(jnp.concatenate([both, rhs], axis=0), y_t, HIGHEST)
+    gram = 0.5 * (first[:width] + dot_nt(y_t, both, HIGHEST))
+    packs = LANES // width
+    tall = width // packs
+    packed = jnp.concatenate([gram[s * tall : (s + 1) * tall] for s in range(packs)], axis=1)
+    sketched = jnp.concatenate([first[width:]] * packs, axis=1)
+    summed = all_reduce(jnp.concatenate([packed, sketched], axis=0), g_plane, g_depth, g_sem)
+    gram = jnp.concatenate([summed[:tall, s * width : (s + 1) * width] for s in range(packs)], axis=0)
+    sketched_rhs = summed[tall:, :width]
+    weights = eliminate(gram, y_t)
+    direction = (rhs - jnp.dot(sketched_rhs, weights, precision=HIGHEST)) / precond_shift
+
+    d_all[me_c] = direction[:1]
+    copies = [
+        send(d_all.at[me_c], d_all.at[me_c], d_sem, t, (me_r, lax.rem(me_c + t, cols)))
+        for t in range(1, cols)
+    ]
+    for copy in copies:
+        copy.wait_recv()
+    for i in range(row_blocks):
+        line = jnp.concatenate([d_all[pieces * i + p] for p in range(pieces)], axis=1)
+        xs[i] = line.astype(jnp.bfloat16).astype(jnp.float32)
+    total = jnp.zeros((16, order), jnp.float32)
+    for n in range(stored):
+        left = spread(xs, brow_ref[n], bcol_ref[n], col_blocks, 16)
+        total = total + jnp.dot(left, vals[n], preferred_element_type=jnp.float32)
+    e_src[...] = total[:8]
+    send(e_src, e_dst, pair_sem, 1, (1 - me_r, me_c)).wait_recv()
+    image_cols = e_src[...] + e_dst[...]
+    for j in range(col_blocks):
+        line = (strip(theta_ref, j) * image_cols[j : j + 1]).astype(jnp.bfloat16)
+        zv[j] = line.astype(jnp.float32)
+    total = jnp.zeros((16, order), jnp.float32)
+    for n in range(stored):
+        left = spread(zv, bcol_ref[n], brow_ref[n], row_blocks, 16)
+        total = total + dot_nt(left, vals[n])
+    for i in range(row_blocks):
+        for p in range(pieces):
+            f_src[pieces * i + p] = total[i : i + 1, p * LANES : (p + 1) * LANES]
+    image = jnp.broadcast_to(scatter_sum(f_src, f_dst, f_sem), (8, LANES)) + regularize * direction
+
+    against = dot_nt(image, y_t, HIGHEST)
+    curvature = jnp.sum(direction * image, axis=1, keepdims=True)
+    along = jnp.sum(rhs * direction, axis=1, keepdims=True)
+    against = jnp.concatenate([against, jnp.zeros((8, LANES - width), jnp.float32)], axis=1)
+    lane = lax.broadcasted_iota(jnp.int32, (8, LANES), 1)
+    value = jnp.where(lane == width, curvature, jnp.where(lane == width + 1, along, against))
+    summed = all_reduce(value, h_plane, h_depth, h_sem)
+    alpha = summed[:, width + 1 : width + 2] / summed[:, width : width + 1]
+    residual = rhs - alpha * image
+    sketched_res = sketched_rhs - alpha * summed[:, :width]
+    pre = (residual - jnp.dot(sketched_res, weights, precision=HIGHEST)) / precond_shift
+    sol_ref[...] = (alpha * direction)[:1]
+    res_ref[...] = residual[:1]
+    pre_ref[...] = pre[:1]
+    for copy in pending:
+        copy.wait_send()
+
+
+def fused(cols, blocks, block_rows, block_cols, sketch, theta, rhs):
+    stored, order = blocks.shape[2], blocks.shape[3]
+    width = sketch.shape[1]
+    row_blocks = sketch.shape[0] // order
+    col_blocks = theta.shape[0] // order
+    depth = cols // PLANE
+    vmem = pl.BlockSpec(memory_space=pltpu.VMEM)
+    smem = pl.BlockSpec(memory_space=pltpu.SMEM)
+    line = jax.ShapeDtypeStruct((1, LANES), jnp.float32)
+    f32 = jnp.float32
+    outs = pl.pallas_call(
+        functools.partial(kernel, cols, row_blocks, col_blocks),
+        out_shape=(line, line, line),
+        in_specs=[smem, smem, pl.BlockSpec(memory_space=pl.ANY), vmem, vmem, vmem],
+        out_specs=(vmem, vmem, vmem),
+        scratch_shapes=[
+            pltpu.VMEM((stored, order, order), jnp.bfloat16),
+            pltpu.VMEM((row_blocks, width, order), f32),
+            pltpu.VMEM((col_blocks * width, order), f32),
+            pltpu.VMEM((col_blocks * width, order), f32),
+            pltpu.VMEM((col_blocks, width, order), f32),
+            pltpu.VMEM((cols, width, LANES), f32),
+            pltpu.VMEM((cols, width, LANES), f32),
+            pltpu.VMEM((2 * PLANE, 16, LANES), f32),
+            pltpu.VMEM((depth, 16, LANES), f32),
+            pltpu.VMEM((cols, 1, LANES), f32),
+            pltpu.VMEM((row_blocks, 1, order), f32),
+            pltpu.VMEM((8, order), f32),
+            pltpu.VMEM((8, order), f32),
+            pltpu.VMEM((col_blocks, 1, order), f32),
+            pltpu.VMEM((cols, 1, LANES), f32),
+            pltpu.VMEM((cols, 1, LANES), f32),
+            pltpu.VMEM((2 * PLANE, 8, LANES), f32),
+            pltpu.VMEM((depth, 8, LANES), f32),
+            pltpu.SemaphoreType.DMA((stored,)),
+            pltpu.SemaphoreType.DMA((2, 2)),
+            pltpu.SemaphoreType.DMA((2, cols)),
+            pltpu.SemaphoreType.DMA((2, 2 * PLANE + depth)),
+            pltpu.SemaphoreType.DMA((2, cols)),
+            pltpu.SemaphoreType.DMA((2, cols)),
+            pltpu.SemaphoreType.DMA((2, 2 * PLANE + depth)),
+        ],
+        compiler_params=pltpu.CompilerParams(
+            collective_id=0, has_side_effects=True, vmem_limit_bytes=32 * 1024 * 1024
+        ),
+    )(
+        block_rows.reshape(stored),
+        block_cols.reshape(stored),
+        blocks.reshape(stored, order, order),
+        sketch,
+        theta.reshape(-1, LANES),
+        rhs.reshape(-1, LANES),
+    )
+    return tuple(out.reshape(LANES) for out in outs)
 
 
 def tile_transpose(values, rows_idx, cols_idx, inputs, col_count):
@@ -102,4 +406,12 @@
         P("row"),
     )
     out_specs = (P(("row", "col")), P(("row", "col")), P(("row", "col")))
-    return jax.shard_map(shards, mesh=mesh, in_specs=in_specs, out_specs=out_specs, check_vma=False)
+    cols = mesh.shape["col"]
+
+    def step(blocks, block_rows, block_cols, sketch, theta, rhs):
+        share = sketch.shape[0] // cols
+        if mesh.shape["row"] == 2 and cols % PLANE == 0 and share == LANES:
+            return fused(cols, blocks, block_rows, block_cols, sketch, theta, rhs)
+        return shards(blocks, block_rows, block_cols, sketch, theta, rhs)
+
+    return jax.shard_map(step, mesh=mesh, in_specs=in_specs, out_specs=out_specs, check_vma=False)

time: 320 us -> 61.4 us (0.19)
  blocking collectives: 156 us -> 0 us
  waiting for transfers between devices: 115 us -> 0 us
  Pallas kernels: 0 us -> 52.9 us
  matrix products: 16.5 us -> 0 us
  between operations: 15.6 us -> 0.66 us
  other arithmetic: 10.6 us -> 0 us
    psum x5 -> x0, blocking collectives: 156 us -> none  [the longest x1 42.5 us: shards(): lax.psum(jnp.dot(residual, y_part, precision=lax.Precision.HIGHEST), ('ro...]
    psum x2 -> x0, waiting for transfers between devices: 115 us -> none  [the longest x1 88.9 us: shards(): ysketch = lax.psum(row_terms, 'col') + regularize * sketch_f]
    pallas_call x0 -> x1, Pallas kernels: none -> 52.9 us  [fused(): pl.pallas_call(functools.partial(kernel, cols, row_blocks, col_blocks), o...]
    dot_general x14 -> x0, matrix products: 15.9 us -> none  [the longest x2 6.87 us: tile_forward(): jnp.einsum('nab,nbk->nak', values, picked, preferred_element_type=jnp.flo...]
    another operation x5 -> x0, other arithmetic: 6.68 us -> none  [the longest x3 3.6 us: shards(): factor = jnp.linalg.cholesky(gram)]
    unnamed x16 -> x14, local copies, waits for them, and re-layouts: 1.61 us -> 7.6 us
  transfers between devices with their start and end apart: 2 -> 0, of which waited for: 2 -> 0; matrix products, arithmetic and copies ran while one was open for 0% -> 0% of each run, Pallas kernels for 0% -> 0%
where the time goes in v1:
time: 61.4 us; the launch traced here: 61.1 us
  Pallas kernels  52.9 us (86%)
  local copies, waits for them, and re-layouts  7.6 us (12%)
  between operations  0.66 us (1%)
    pallas_call x1, Pallas kernels, fused(): pl.pallas_call(functools.partial(kernel, cols, row_blocks, col_blocks), o...  52.9 us
    unnamed x14, local copies, waits for them, and re-layouts  7.6 us

profile of v1, /device:TPU:0, one launch (start us, length us, event | category | flops | bytes accessed | tf_op | source)
XLA Modules:
  0.0 61.1 jit_solution(4373680038233283940)
XLA Ops:
  0.6 1.2 %copy.9.sketch_ref = bf16[2048,32]{1,0:T(8,128)(2,1)S(1)} copy(bf16[2048,32]{0,1:T(8,128)(2,1)} %param.9) | data formatting | bytes 262144 | tf_op args[3]
  1.8 0.0 copy-start
  1.8 2.2 %copy-done = bf16[1,1,8,512,512]{4,3,2,1,0:T(8,128)(2,1)S(1)} copy-done((bf16[1,1,8,512,512]{4,3,2,1,0:T(8,128)(2,1)S(1)}, bf16[1,1,8,512,512]{4,3,2,1,0:T(8,128)(2,1)}, u32[]{:S(2)}) %copy-start) | copy-done | bytes 4194328
  4.0 0.0 copy-start.1
  4.0 0.7 %copy-done.1 = f32[2048]{0:T(1024)S(1)} copy-done((f32[2048]{0:T(1024)S(1)}, f32[2048]{0:T(1024)}, u32[]{:S(2)}) %copy-start.1) | copy-done | bytes 8216
  4.7 0.0 copy-start.2
  4.7 0.7 %copy-done.2 = f32[2048]{0:T(1024)S(1)} copy-done((f32[2048]{0:T(1024)S(1)}, f32[2048]{0:T(1024)}, u32[]{:S(2)}) %copy-start.2) | copy-done | bytes 8216
  5.4 0.0 copy-start.3
  5.4 0.7 %copy-done.3 = s32[1,1,8]{2,1,0:T(1,128)S(1)} copy-done((s32[1,1,8]{2,1,0:T(1,128)S(1)}, s32[1,1,8]{2,1,0:T(1,128)}, u32[]{:S(2)}) %copy-start.3) | copy-done | bytes 56
  6.1 0.0 copy-start.4
  6.1 0.7 %copy-done.4 = s32[1,1,8]{2,1,0:T(1,128)S(1)} copy-done((s32[1,1,8]{2,1,0:T(1,128)S(1)}, s32[1,1,8]{2,1,0:T(1,128)}, u32[]{:S(2)}) %copy-start.4) | copy-done | bytes 56
  6.7 52.9 %shard_map.85 = (f32[1,128]{1,0:T(1,128)S(1)}, f32[1,128]{1,0:T(1,128)S(1)}, f32[1,128]{1,0:T(1,128)S(1)}) custom-call(s32[8]{0:T(128)S(1)} %bitcast.11, s32[8]{0:T(128)S(1)} %bitcast.12, bf16[8,512,512]{2,1,0:T(8,128)(2,1)S(1)} %bitcast.8, bf16[2048,32]{1,0:T(8,128)(2,1)S(1)} %copy.9.sketch_ref, f32[16,128]{1,0:T(8,128)S(1)} %bitcast.9, f32[16,128]{1,0:T(8,128)S(1)} %bitcast.10), custom_call_target="tpu_custom_call" | custom-call | tf_op jit(solution)/shard_map/pallas_call | solution.py:268
  59.6 0.5 copy.13
  60.1 0.5 copy.14
  60.6 0.5 copy.15
Async XLA Ops:
  1.8 2.2 %copy-start = (bf16[1,1,8,512,512]{4,3,2,1,0:T(8,128)(2,1)S(1)}, bf16[1,1,8,512,512]{4,3,2,1,0:T(8,128)(2,1)}, u32[]{:S(2)}) copy-start(bf16[1,1,8,512,512]{4,3,2,1,0:T(8,128)(2,1)} %param.6) | copy-start | bytes 12582916
  4.0 0.7 %copy-start.1 = (f32[2048]{0:T(1024)S(1)}, f32[2048]{0:T(1024)}, u32[]{:S(2)}) copy-start(f32[2048]{0:T(1024)} %param.10) | copy-start | bytes 24580
  4.7 0.7 %copy-start.2 = (f32[2048]{0:T(1024)S(1)}, f32[2048]{0:T(1024)}, u32[]{:S(2)}) copy-start(f32[2048]{0:T(1024)} %param.11) | copy-start | bytes 24580
  5.4 0.7 %copy-start.3 = (s32[1,1,8]{2,1,0:T(1,128)S(1)}, s32[1,1,8]{2,1,0:T(1,128)}, u32[]{:S(2)}) copy-start(s32[1,1,8]{2,1,0:T(1,128)} %param.7) | copy-start | bytes 100
  6.1 0.7 %copy-start.4 = (s32[1,1,8]{2,1,0:T(1,128)S(1)}, s32[1,1,8]{2,1,0:T(1,128)}, u32[]{:S(2)}) copy-start(s32[1,1,8]{2,1,0:T(1,128)} %param.8) | copy-start | bytes 100

commit v2 on v1

--- a/solution.py
+++ b/solution.py
@@ -13,6 +13,7 @@
 HIGHEST = lax.Precision.HIGHEST
 PLANE = 4
 LANES = 128
+VMEM_BYTES = 64 * 1024 * 1024
 
 
 def dot_nt(left, right, precision=None):
@@ -32,43 +33,59 @@
     return jnp.where(group == place, tall, 0.0).astype(jnp.bfloat16)
 
 
-def eliminate(matrix, right):
+def eliminate(matrix):
     order = matrix.shape[0]
-    matrix = jnp.concatenate([matrix, jnp.zeros((order, LANES - order), jnp.float32)], axis=1)
+    panel = 8
     at = lax.broadcasted_iota(jnp.int32, (order, LANES), 0)
-    for k in range(order):
-        inverse = 1.0 / matrix[k : k + 1, k : k + 1]
-        column = jnp.broadcast_to(matrix[:, k : k + 1], (order, LANES))
-        row_m = matrix[k : k + 1, :] * inverse
-        row_r = right[k : k + 1, :] * inverse
-        matrix = jnp.where(at == k, row_m, matrix - column * row_m)
-        right = jnp.where(at == k, row_r, right - column * row_r)
-    return right
+    lane = lax.broadcasted_iota(jnp.int32, (order, LANES), 1)
+    rest = LANES - matrix.shape[1]
+    wide = jnp.concatenate([matrix, jnp.zeros((order, rest), jnp.float32)], axis=1)
+    wide = jnp.where(lane == at + 2 * order, 1.0, wide)
+    for start in range(0, order, panel):
+        columns = [
+            jnp.broadcast_to(wide[:, k : k + 1], (order, LANES)) for k in range(start, start + panel)
+        ]
+        for j in range(panel):
+            k = start + j
+            here = at == k
+            column = columns[j]
+            inverse = 1.0 / column[k : k + 1]
+            for other in range(j + 1, panel):
+                row = columns[other][k : k + 1] * inverse
+                columns[other] = jnp.where(here, row, columns[other] - column * row)
+            row = wide[k : k + 1] * inverse
+            wide = jnp.where(here, row, wide - column * row)
+    return wide[:, order : order + 1], wide[:, 2 * order : 3 * order]
 
 
 def kernel(
     cols,
     row_blocks,
     col_blocks,
+    brow_hbm,
+    bcol_hbm,
+    blocks_ref,
+    sketch_hbm,
+    theta_hbm,
+    rhs_hbm,
+    out_ref,
     brow_ref,
     bcol_ref,
-    blocks_ref,
     sketch_ref,
     theta_ref,
     rhs_ref,
-    sol_ref,
-    res_ref,
-    pre_ref,
     vals,
     sk_t,
     s_src,
     s_dst,
     zs,
+    y_own,
+    y_pair,
     y_src,
     y_dst,
+    y_all,
     g_plane,
     g_depth,
-    d_all,
     xs,
     e_src,
     e_dst,
@@ -77,28 +94,43 @@
     f_dst,
     h_plane,
     h_depth,
-    block_sem,
+    load_sem,
     pair_sem,
     y_sem,
+    a_sem,
     g_sem,
-    d_sem,
     f_sem,
     h_sem,
 ):
     me_r = lax.axis_index("row")
     me_c = lax.axis_index("col")
     stored, order = vals.shape[0], vals.shape[1]
-    width = sketch_ref.shape[1]
+    width = sketch_ref.shape[0]
     pieces = order // LANES
     depth = cols // PLANE
     z, q = me_c // PLANE, me_c % PLANE
     plane = 2 * PLANE
     me_p = me_r * PLANE + q
+    core, chip, chips = lax.rem(me_c, 2), me_c // 2, cols // 2
+    twin = (me_r, chip * 2 + 1 - core)
     pending = []
 
+    smalls = []
+    for at, (src, dst) in enumerate(
+        [
+            (sketch_hbm, sketch_ref),
+            (brow_hbm, brow_ref),
+            (bcol_hbm, bcol_ref),
+            (theta_hbm, theta_ref),
+            (rhs_hbm, rhs_ref),
+        ]
+    ):
+        load = pltpu.make_async_copy(src, dst, load_sem.at[stored + at])
+        load.start()
+        smalls.append(load)
     loads = []
     for n in range(stored):
-        load = pltpu.make_async_copy(blocks_ref.at[n], vals.at[n], block_sem.at[n])
+        load = pltpu.make_async_copy(blocks_ref.at[n], vals.at[n], load_sem.at[n])
         load.start()
         loads.append(load)
 
@@ -125,13 +157,16 @@
         pending.append(copy)
         return copy
 
-    def all_reduce(value, first, second, sems):
+    def reduce_start(value, first, sems):
         first[me_p] = value
         copies = []
         for u in range(1, plane):
             peer = lax.rem(me_p + u, plane)
             device = (peer // PLANE, z * PLANE + lax.rem(peer, PLANE))
             copies.append(send(first.at[me_p], first.at[me_p], sems, u - 1, device))
+        return copies
+
+    def reduce_middle(copies, first, second, sems):
         for copy in copies:
             copy.wait_recv()
         total = first[0]
@@ -142,6 +177,9 @@
         for u in range(1, depth):
             device = (me_r, lax.rem(z + u, depth) * PLANE + q)
             copies.append(send(second.at[z], second.at[z], sems, plane - 2 + u, device))
+        return copies
+
+    def reduce_finish(copies, second):
         for copy in copies:
             copy.wait_recv()
         total = second[0]
@@ -149,12 +187,14 @@
             total = total + second[u]
         return total
 
-    def scatter_sum(src, dst, sems):
+    def scatter_start(src, dst, sems):
         copies = []
         for t in range(1, cols):
             to = lax.rem(me_c + t, cols)
             copies.append(send(src.at[to], dst.at[t], sems, t, (me_r, to)))
-        total = src[me_c]
+        return copies
+
+    def scatter_finish(total, copies, dst):
         for t, copy in enumerate(copies, 1):
             copy.wait_recv()
             total = total + dst[t]
@@ -163,67 +203,105 @@
     def strip(ref, j):
         return jnp.concatenate([ref[pieces * j + p : pieces * j + p + 1, :] for p in range(pieces)], axis=1)
 
-    eye = (
-        lax.broadcasted_iota(jnp.int32, (width, width), 0)
-        == lax.broadcasted_iota(jnp.int32, (width, width), 1)
-    )
-    eye = jnp.where(eye, 1.0, 0.0).astype(jnp.bfloat16)
+    for load in smalls:
+        load.wait()
     for i in range(row_blocks):
-        sk_t[i] = dot_nt(eye, sketch_ref[i * order : (i + 1) * order, :])
-    omega = dot_nt(eye, sketch_ref[pl.ds(pl.multiple_of(me_c * LANES, LANES), LANES), :])
+        sk_t[i] = sketch_ref[:, i * order : (i + 1) * order].astype(jnp.float32)
+    own = pl.ds(pl.multiple_of(me_c * LANES, LANES), LANES)
+    omega = sketch_ref[:, own].astype(jnp.float32)
     rhs = jnp.broadcast_to(rhs_ref[pl.ds(me_c, 1), :], (8, LANES))
 
-    total = jnp.zeros((col_blocks * width, order), jnp.float32)
-    for n in range(stored):
-        left = spread(sk_t, brow_ref[n], bcol_ref[n], col_blocks, col_blocks * width)
-        loads[n].wait()
-        total = total + jnp.dot(left, vals[n], preferred_element_type=jnp.float32)
-    s_src[...] = total
-    pl.semaphore_wait(barrier, cols - 1 + PLANE)
-    send(s_src, s_dst, pair_sem, 0, (1 - me_r, me_c)).wait_recv()
-    for j in range(col_blocks):
-        part = slice(j * width, (j + 1) * width)
-        scaled = (strip(theta_ref, j) * (s_src[part, :] + s_dst[part, :])).astype(jnp.bfloat16)
-        zs[j] = scaled.astype(jnp.float32)
-
+    halves = 2
+    half = order // halves
+    lefts = [
+        spread(sk_t, brow_ref[n], bcol_ref[n], col_blocks, col_blocks * width) for n in range(stored)
+    ]
+    mine, copies = [], []
+    for h in range(halves):
+        part = slice(h * half, (h + 1) * half)
+        total = jnp.zeros((col_blocks * width, half), jnp.float32)
+        for n in range(stored):
+            if h == 0:
+                loads[n].wait()
+            total = total + jnp.dot(lefts[n], vals[n, :, part], preferred_element_type=jnp.float32)
+        s_src[h] = total.astype(jnp.bfloat16)
+        mine.append(total)
+        if h == 0:
+            pl.semaphore_wait(barrier, cols - 1 + PLANE)
+        copies.append(send(s_src.at[h], s_dst.at[h], pair_sem, h, (1 - me_r, me_c)))
     total = jnp.zeros((row_blocks * width, order), jnp.float32)
-    for n in range(stored):
-        left = spread(zs, bcol_ref[n], brow_ref[n], row_blocks, row_blocks * width)
-        total = total + dot_nt(left, vals[n])
+    for h in range(halves):
+        part = slice(h * half, (h + 1) * half)
+        copies[h].wait_recv()
+        summed = mine[h] + s_dst[h].astype(jnp.float32)
+        for j in range(col_blocks):
+            scaled = strip(theta_ref, j)[:, part] * summed[j * width : (j + 1) * width]
+            zs[h, j] = scaled.astype(jnp.bfloat16).astype(jnp.float32)
+        for n in range(stored):
+            left = spread(zs.at[h], bcol_ref[n], brow_ref[n], row_blocks, row_blocks * width)
+            total = total + dot_nt(left, vals[n, :, part])
     for i in range(row_blocks):
         for p in range(pieces):
-            y_src[pieces * i + p] = total[i * width : (i + 1) * width, p * LANES : (p + 1) * LANES]
-    y_t = scatter_sum(y_src, y_dst, y_sem) + regularize * omega
+            at = pieces * i + p
+            y_own[at % 2, at // 2] = total[i * width : (i + 1) * width, p * LANES : (p + 1) * LANES]
+    copy = send(y_own.at[1 - core], y_pair, pair_sem, halves, twin)
+    copy.wait_recv()
+    for t in range(chips):
+        y_src[t] = y_own[core, t] + y_pair[t]
+    copies = []
+    for t in range(1, chips):
+        to = lax.rem(chip + t, chips)
+        copies.append(send(y_src.at[to], y_dst.at[t], y_sem, t, (me_r, to * 2 + core)))
+    y_t = scatter_finish(y_src[chip] + regularize * omega, copies, y_dst)
+    y_all[core, chip] = y_t
 
     both = y_t + precond_shift * omega
-    first = dot_nt(jnp.concatenate([both, rhs], axis=0), y_t, HIGHEST)
-    gram = 0.5 * (first[:width] + dot_nt(y_t, both, HIGHEST))
-    packs = LANES // width
+    tall_rhs = jnp.broadcast_to(rhs[:1], (width, LANES))
+    upper = jnp.concatenate([0.5 * y_t, 0.5 * both], axis=1)
+    lower = jnp.concatenate([jnp.zeros((width, LANES), jnp.float32), tall_rhs], axis=1)
+    joined = dot_nt(
+        jnp.concatenate([both, y_t], axis=1), jnp.concatenate([upper, lower], axis=0), HIGHEST
+    )
+    packs = LANES // (2 * width)
     tall = width // packs
-    packed = jnp.concatenate([gram[s * tall : (s + 1) * tall] for s in range(packs)], axis=1)
-    sketched = jnp.concatenate([first[width:]] * packs, axis=1)
-    summed = all_reduce(jnp.concatenate([packed, sketched], axis=0), g_plane, g_depth, g_sem)
-    gram = jnp.concatenate([summed[:tall, s * width : (s + 1) * width] for s in range(packs)], axis=0)
-    sketched_rhs = summed[tall:, :width]
-    weights = eliminate(gram, y_t)
-    direction = (rhs - jnp.dot(sketched_rhs, weights, precision=HIGHEST)) / precond_shift
-
-    d_all[me_c] = direction[:1]
-    copies = [
-        send(d_all.at[me_c], d_all.at[me_c], d_sem, t, (me_r, lax.rem(me_c + t, cols)))
-        for t in range(1, cols)
-    ]
-    for copy in copies:
+    packed = jnp.concatenate([joined[s * tall : (s + 1) * tall] for s in range(packs)], axis=1)
+    copies = reduce_start(packed, g_plane, g_sem)
+    gathers = []
+    for t in range(1, chips):
+        to = lax.rem(chip + t, chips)
+        gathers.append(send(y_all.at[core, chip], y_all.at[core, chip], a_sem, t, (me_r, to * 2 + core)))
+    copies = reduce_middle(copies, g_plane, g_depth, g_sem)
+    for copy in gathers:
         copy.wait_recv()
+    gathered = send(y_all.at[core], y_all.at[core], a_sem, 0, twin)
+    summed = reduce_finish(copies, g_depth)
+    joined = jnp.concatenate(
+        [summed[:, s * 2 * width : (s + 1) * 2 * width] for s in range(packs)], axis=0
+    )
+    sketched_rhs = joined[:, width : width + 1]
+    coeffs, inverse = eliminate(joined)
+    coeffs = jnp.broadcast_to(coeffs, (width, LANES))
+    taken = jnp.sum(coeffs * y_t, axis=0, keepdims=True)
+    direction = (rhs[:1] - taken) / precond_shift
+
+    gathered.wait_recv()
+    lines = []
     for i in range(row_blocks):
-        line = jnp.concatenate([d_all[pieces * i + p] for p in range(pieces)], axis=1)
+        taken = []
+        for p in range(pieces):
+            at = pieces * i + p
+            taken.append(jnp.sum(coeffs * y_all[at % 2, at // 2], axis=0, keepdims=True))
+        line = (strip(rhs_ref, i) - jnp.concatenate(taken, axis=1)) / precond_shift
+        lines.append(line)
         xs[i] = line.astype(jnp.bfloat16).astype(jnp.float32)
     total = jnp.zeros((16, order), jnp.float32)
     for n in range(stored):
         left = spread(xs, brow_ref[n], bcol_ref[n], col_blocks, 16)
         total = total + jnp.dot(left, vals[n], preferred_element_type=jnp.float32)
     e_src[...] = total[:8]
-    send(e_src, e_dst, pair_sem, 1, (1 - me_r, me_c)).wait_recv()
+    copy = send(e_src, e_dst, pair_sem, halves + 1, (1 - me_r, me_c))
+    weights = jnp.dot(inverse, y_t, precision=HIGHEST)
+    copy.wait_recv()
     image_cols = e_src[...] + e_dst[...]
     for j in range(col_blocks):
         line = (strip(theta_ref, j) * image_cols[j : j + 1]).astype(jnp.bfloat16)
@@ -232,83 +310,107 @@
     for n in range(stored):
         left = spread(zv, bcol_ref[n], brow_ref[n], row_blocks, 16)
         total = total + dot_nt(left, vals[n])
+
+    against = regularize * y_t * direction
+    curvature = regularize * direction * direction
     for i in range(row_blocks):
         for p in range(pieces):
-            f_src[pieces * i + p] = total[i : i + 1, p * LANES : (p + 1) * LANES]
-    image = jnp.broadcast_to(scatter_sum(f_src, f_dst, f_sem), (8, LANES)) + regularize * direction
-
-    against = dot_nt(image, y_t, HIGHEST)
-    curvature = jnp.sum(direction * image, axis=1, keepdims=True)
-    along = jnp.sum(rhs * direction, axis=1, keepdims=True)
-    against = jnp.concatenate([against, jnp.zeros((8, LANES - width), jnp.float32)], axis=1)
-    lane = lax.broadcasted_iota(jnp.int32, (8, LANES), 1)
+            part = slice(p * LANES, (p + 1) * LANES)
+            piece = total[i : i + 1, part]
+            f_src[pieces * i + p] = piece
+            against = against + y_all[(pieces * i + p) % 2, (pieces * i + p) // 2] * piece
+            curvature = curvature + lines[i][:, part] * piece
+    at = lax.broadcasted_iota(jnp.int32, (width, LANES), 0)
+    diagonal = lax.broadcasted_iota(jnp.int32, (width, LANES), 1) == at
+    against = jnp.where(diagonal, jnp.sum(against, axis=1, keepdims=True), 0.0)
+    against = jnp.sum(against, axis=0, keepdims=True)
+    curvature = jnp.sum(curvature, axis=1, keepdims=True)
+    along = jnp.sum(rhs[:1] * direction, axis=1, keepdims=True)
+    lane = lax.broadcasted_iota(jnp.int32, (1, LANES), 1)
     value = jnp.where(lane == width, curvature, jnp.where(lane == width + 1, along, against))
-    summed = all_reduce(value, h_plane, h_depth, h_sem)
+    copies = reduce_start(value, h_plane, h_sem)
+    scatters = scatter_start(f_src, f_dst, f_sem)
+    copies = reduce_middle(copies, h_plane, h_depth, h_sem)
+    image = scatter_finish(f_src[me_c], scatters, f_dst)
+    summed = reduce_finish(copies, h_depth)
     alpha = summed[:, width + 1 : width + 2] / summed[:, width : width + 1]
-    residual = rhs - alpha * image
-    sketched_res = sketched_rhs - alpha * summed[:, :width]
-    pre = (residual - jnp.dot(sketched_res, weights, precision=HIGHEST)) / precond_shift
-    sol_ref[...] = (alpha * direction)[:1]
-    res_ref[...] = residual[:1]
-    pre_ref[...] = pre[:1]
+    sketched = jnp.sum(jnp.where(diagonal, summed, 0.0), axis=1, keepdims=True)
+    taken = jnp.sum((sketched_rhs - alpha * sketched) * weights, axis=0, keepdims=True)
+    out_ref[0:1] = jnp.broadcast_to(alpha, (1, LANES))
+    out_ref[1:2] = direction
+    out_ref[2:3] = rhs[:1]
+    out_ref[3:4] = image
+    out_ref[4:5] = taken
+    out_ref[5:8] = jnp.zeros((3, LANES), jnp.float32)
     for copy in pending:
         copy.wait_send()
 
 
 def fused(cols, blocks, block_rows, block_cols, sketch, theta, rhs):
     stored, order = blocks.shape[2], blocks.shape[3]
-    width = sketch.shape[1]
-    row_blocks = sketch.shape[0] // order
+    local, width = sketch.shape
+    row_blocks = local // order
     col_blocks = theta.shape[0] // order
     depth = cols // PLANE
     vmem = pl.BlockSpec(memory_space=pltpu.VMEM)
-    smem = pl.BlockSpec(memory_space=pltpu.SMEM)
-    line = jax.ShapeDtypeStruct((1, LANES), jnp.float32)
-    f32 = jnp.float32
-    outs = pl.pallas_call(
+    hbm = pl.BlockSpec(memory_space=pl.ANY)
+    f32, bf16 = jnp.float32, jnp.bfloat16
+    reduce_sems = pltpu.SemaphoreType.DMA((2, 2 * PLANE + depth))
+    col_sems = pltpu.SemaphoreType.DMA((2, cols))
+    out = pl.pallas_call(
         functools.partial(kernel, cols, row_blocks, col_blocks),
-        out_shape=(line, line, line),
-        in_specs=[smem, smem, pl.BlockSpec(memory_space=pl.ANY), vmem, vmem, vmem],
-        out_specs=(vmem, vmem, vmem),
+        out_shape=jax.ShapeDtypeStruct((8, LANES), jnp.float32),
+        in_specs=[hbm] * 6,
+        out_specs=vmem,
         scratch_shapes=[
-            pltpu.VMEM((stored, order, order), jnp.bfloat16),
+            pltpu.SMEM((stored,), jnp.int32),
+            pltpu.SMEM((stored,), jnp.int32),
+            pltpu.VMEM((width, local), bf16),
+            pltpu.VMEM((theta.shape[0] // LANES, LANES), f32),
+            pltpu.VMEM((local // LANES, LANES), f32),
+            pltpu.VMEM((stored, order, order), bf16),
             pltpu.VMEM((row_blocks, width, order), f32),
-            pltpu.VMEM((col_blocks * width, order), f32),
-            pltpu.VMEM((col_blocks * width, order), f32),
-            pltpu.VMEM((col_blocks, width, order), f32),
-            pltpu.VMEM((cols, width, LANES), f32),
-            pltpu.VMEM((cols, width, LANES), f32),
+            pltpu.VMEM((2, col_blocks * width, order // 2), bf16),
+            pltpu.VMEM((2, col_blocks * width, order // 2), bf16),
+            pltpu.VMEM((2, col_blocks, width, order // 2), f32),
+            pltpu.VMEM((2, cols // 2, width, LANES), f32),
+            pltpu.VMEM((cols // 2, width, LANES), f32),
+            pltpu.VMEM((cols // 2, width, LANES), f32),
+            pltpu.VMEM((cols // 2, width, LANES), f32),
+            pltpu.VMEM((2, cols // 2, width, LANES), f32),
             pltpu.VMEM((2 * PLANE, 16, LANES), f32),
             pltpu.VMEM((depth, 16, LANES), f32),
-            pltpu.VMEM((cols, 1, LANES), f32),
             pltpu.VMEM((row_blocks, 1, order), f32),
             pltpu.VMEM((8, order), f32),
             pltpu.VMEM((8, order), f32),
             pltpu.VMEM((col_blocks, 1, order), f32),
             pltpu.VMEM((cols, 1, LANES), f32),
             pltpu.VMEM((cols, 1, LANES), f32),
-            pltpu.VMEM((2 * PLANE, 8, LANES), f32),
-            pltpu.VMEM((depth, 8, LANES), f32),
-            pltpu.SemaphoreType.DMA((stored,)),
-            pltpu.SemaphoreType.DMA((2, 2)),
-            pltpu.SemaphoreType.DMA((2, cols)),
-            pltpu.SemaphoreType.DMA((2, 2 * PLANE + depth)),
-            pltpu.SemaphoreType.DMA((2, cols)),
-            pltpu.SemaphoreType.DMA((2, cols)),
-            pltpu.SemaphoreType.DMA((2, 2 * PLANE + depth)),
+            pltpu.VMEM((2 * PLANE, 1, LANES), f32),
+            pltpu.VMEM((depth, 1, LANES), f32),
+            pltpu.SemaphoreType.DMA((stored + 5,)),
+            pltpu.SemaphoreType.DMA((2, 4)),
+            col_sems,
+            col_sems,
+            reduce_sems,
+            col_sems,
+            reduce_sems,
         ],
         compiler_params=pltpu.CompilerParams(
-            collective_id=0, has_side_effects=True, vmem_limit_bytes=32 * 1024 * 1024
+            collective_id=0, has_side_effects=True, vmem_limit_bytes=VMEM_BYTES
         ),
     )(
         block_rows.reshape(stored),
         block_cols.reshape(stored),
         blocks.reshape(stored, order, order),
-        sketch,
+        sketch.T,
         theta.reshape(-1, LANES),
         rhs.reshape(-1, LANES),
     )
-    return tuple(out.reshape(LANES) for out in outs)
+    alpha, direction, mine, image, taken = (out[i] for i in range(5))
+    iterate = alpha * direction
+    residual = mine - alpha * image - regularize * iterate
+    return iterate, residual, (residual - taken) / precond_shift
 
 
 def tile_transpose(values, rows_idx, cols_idx, inputs, col_count):

time: 61.4 us -> 42 us (0.68)
  Pallas kernels: 52.9 us -> 39.8 us
  local copies, waits for them, and re-layouts: 7.6 us -> 0 us
  other arithmetic: 0 us -> 1.38 us
    pallas_call x1, Pallas kernels: 52.9 us -> 39.8 us  [fused(): pl.pallas_call(functools.partial(kernel, cols, row_blocks, col_blocks), o...]
    unnamed x14 -> x0, local copies, waits for them, and re-layouts: 7.6 us -> none
    sub x0 -> x1, other arithmetic: none -> 1.38 us  [fused(): return (iterate, residual, (residual - taken) / precond_shift)]
where the time goes in v2:
time: 42 us; the launch traced here: 41.9 us
  Pallas kernels  39.8 us (95%)
  other arithmetic  1.38 us (3%)
  between operations  0.64 us (2%)
    pallas_call x1, Pallas kernels, fused(): pl.pallas_call(functools.partial(kernel, cols, row_blocks, col_blocks), o...  39.8 us
    sub x1, other arithmetic, fused(): return (iterate, residual, (residual - taken) / precond_shift)  1.38 us

profile of v2, /device:TPU:0, one launch (start us, length us, event | category | flops | bytes accessed | tf_op | source)
XLA Modules:
  0.0 41.9 jit_solution(2818133165197937582)
XLA Ops:
  0.6 39.8 %shard_map.85 = f32[8,128]{1,0:T(8,128)} custom-call(s32[8]{0:T(128)} %bitcast.18, s32[8]{0:T(128)} %bitcast.19, bf16[8,512,512]{2,1,0:T(8,128)(2,1)} %bitcast.14, bf16[32,2048]{1,0:T(8,128)(2,1)} %bitcast.15, f32[16,128]{1,0:T(8,128)} %bitcast.16, f32[16,128]{1,0:T(8,128)} %bitcast.17), custom_call_target="tpu_custom_call" | custom-call | tf_op jit(solution)/shard_map/pallas_call | solution.py:360
  40.5 1.4 %bitcast_subtract_fusion = (f32[128]{0:T(128)}, f32[128]{0:T(128)}, f32[128]{0:T(128)}) fusion(f32[8,128]{1,0:T(8,128)} %shard_map.85), kind=kLoop, calls=%fused_computation | loop fusion | flops 768 | bytes 4096 | tf_op jit(solution)/shard_map/sub | solution.py:413

commit v3 on v2

--- a/solution.py
+++ b/solution.py
@@ -92,15 +92,14 @@
     zv,
     f_src,
     f_dst,
-    h_plane,
-    h_depth,
+    h_src,
+    h_dst,
     load_sem,
     pair_sem,
     y_sem,
     a_sem,
     g_sem,
     f_sem,
-    h_sem,
 ):
     me_r = lax.axis_index("row")
     me_c = lax.axis_index("col")
@@ -186,13 +185,6 @@
         for u in range(1, depth):
             total = total + second[u]
         return total
-
-    def scatter_start(src, dst, sems):
-        copies = []
-        for t in range(1, cols):
-            to = lax.rem(me_c + t, cols)
-            copies.append(send(src.at[to], dst.at[t], sems, t, (me_r, to)))
-        return copies
 
     def scatter_finish(total, copies, dst):
         for t, copy in enumerate(copies, 1):
@@ -254,6 +246,10 @@
         copies.append(send(y_src.at[to], y_dst.at[t], y_sem, t, (me_r, to * 2 + core)))
     y_t = scatter_finish(y_src[chip] + regularize * omega, copies, y_dst)
     y_all[core, chip] = y_t
+    gathers = []
+    for t in range(1, chips):
+        to = lax.rem(chip + t, chips)
+        gathers.append(send(y_all.at[core, chip], y_all.at[core, chip], a_sem, t, (me_r, to * 2 + core)))
 
     both = y_t + precond_shift * omega
     tall_rhs = jnp.broadcast_to(rhs[:1], (width, LANES))
@@ -266,10 +262,6 @@
     tall = width // packs
     packed = jnp.concatenate([joined[s * tall : (s + 1) * tall] for s in range(packs)], axis=1)
     copies = reduce_start(packed, g_plane, g_sem)
-    gathers = []
-    for t in range(1, chips):
-        to = lax.rem(chip + t, chips)
-        gathers.append(send(y_all.at[core, chip], y_all.at[core, chip], a_sem, t, (me_r, to * 2 + core)))
     copies = reduce_middle(copies, g_plane, g_depth, g_sem)
     for copy in gathers:
         copy.wait_recv()
@@ -317,7 +309,7 @@
         for p in range(pieces):
             part = slice(p * LANES, (p + 1) * LANES)
             piece = total[i : i + 1, part]
-            f_src[pieces * i + p] = piece
+            f_src[pieces * i + p, 0:1] = piece
             against = against + y_all[(pieces * i + p) % 2, (pieces * i + p) // 2] * piece
             curvature = curvature + lines[i][:, part] * piece
     at = lax.broadcasted_iota(jnp.int32, (width, LANES), 0)
@@ -328,11 +320,18 @@
     along = jnp.sum(rhs[:1] * direction, axis=1, keepdims=True)
     lane = lax.broadcasted_iota(jnp.int32, (1, LANES), 1)
     value = jnp.where(lane == width, curvature, jnp.where(lane == width + 1, along, against))
-    copies = reduce_start(value, h_plane, h_sem)
-    scatters = scatter_start(f_src, f_dst, f_sem)
-    copies = reduce_middle(copies, h_plane, h_depth, h_sem)
-    image = scatter_finish(f_src[me_c], scatters, f_dst)
-    summed = reduce_finish(copies, h_depth)
+    for to in range(cols):
+        f_src[to, 1:2] = value
+    copies = []
+    for t in range(1, cols):
+        to = lax.rem(me_c + t, cols)
+        copies.append(send(f_src.at[to], f_dst.at[t], f_sem, t, (me_r, to)))
+    gathered = scatter_finish(f_src[me_c], copies, f_dst)
+    h_src[...] = gathered
+    copy = send(h_src, h_dst, pair_sem, halves + 2, (1 - me_r, me_c))
+    image = gathered[0:1]
+    copy.wait_recv()
+    summed = gathered[1:2] + h_dst[1:2]
     alpha = summed[:, width + 1 : width + 2] / summed[:, width : width + 1]
     sketched = jnp.sum(jnp.where(diagonal, summed, 0.0), axis=1, keepdims=True)
     taken = jnp.sum((sketched_rhs - alpha * sketched) * weights, axis=0, keepdims=True)
@@ -384,17 +383,16 @@
             pltpu.VMEM((8, order), f32),
             pltpu.VMEM((8, order), f32),
             pltpu.VMEM((col_blocks, 1, order), f32),
-            pltpu.VMEM((cols, 1, LANES), f32),
-            pltpu.VMEM((cols, 1, LANES), f32),
-            pltpu.VMEM((2 * PLANE, 1, LANES), f32),
-            pltpu.VMEM((depth, 1, LANES), f32),
+            pltpu.VMEM((cols, 2, LANES), f32),
+            pltpu.VMEM((cols, 2, LANES), f32),
+            pltpu.VMEM((2, LANES), f32),
+            pltpu.VMEM((2, LANES), f32),
             pltpu.SemaphoreType.DMA((stored + 5,)),
-            pltpu.SemaphoreType.DMA((2, 4)),
+            pltpu.SemaphoreType.DMA((2, 5)),
             col_sems,
             col_sems,
             reduce_sems,
             col_sems,
-            reduce_sems,
         ],
         compiler_params=pltpu.CompilerParams(
             collective_id=0, has_side_effects=True, vmem_limit_bytes=VMEM_BYTES

time: 42 us -> 42.2 us (level)
  no operation moved by 1% of the time
where the time goes in v3:
time: 42.2 us; the launch traced here: 42.1 us
  Pallas kernels  40.1 us (95%)
  other arithmetic  1.38 us (3%)
  between operations  0.64 us (2%)
    pallas_call x1, Pallas kernels, fused(): pl.pallas_call(functools.partial(kernel, cols, row_blocks, col_blocks), o...  40.1 us
    sub x1, other arithmetic, fused(): return (iterate, residual, (residual - taken) / precond_shift)  1.38 us

profile of v3, /device:TPU:0, one launch (start us, length us, event | category | flops | bytes accessed | tf_op | source)
XLA Modules:
  0.0 42.1 jit_solution(10807307904346752857)
XLA Ops:
  0.6 40.1 %shard_map.85 = f32[8,128]{1,0:T(8,128)} custom-call(s32[8]{0:T(128)} %bitcast.18, s32[8]{0:T(128)} %bitcast.19, bf16[8,512,512]{2,1,0:T(8,128)(2,1)} %bitcast.14, bf16[32,2048]{1,0:T(8,128)(2,1)} %bitcast.15, f32[16,128]{1,0:T(8,128)} %bitcast.16, f32[16,128]{1,0:T(8,128)} %bitcast.17), custom_call_target="tpu_custom_call" | custom-call | tf_op jit(solution)/shard_map/pallas_call | solution.py:359
  40.7 1.4 %bitcast_subtract_fusion = (f32[128]{0:T(128)}, f32[128]{0:T(128)}, f32[128]{0:T(128)}) fusion(f32[8,128]{1,0:T(8,128)} %shard_map.85), kind=kLoop, calls=%fused_computation | loop fusion | flops 768 | bytes 4096 | tf_op jit(solution)/shard_map/sub | solution.py:411

commit v4 on v3

--- a/solution.py
+++ b/solution.py
@@ -31,6 +31,12 @@
         tall = jnp.concatenate([picked] * copies, axis=0)
     group = lax.broadcasted_iota(jnp.int32, (height, lanes), 0) // width
     return jnp.where(group == place, tall, 0.0).astype(jnp.bfloat16)
+
+
+def spread_lanes(source, index, place, width):
+    picked = source[index]
+    group = lax.broadcasted_iota(jnp.int32, picked.shape, 1) // width
+    return jnp.where(group == place, picked, 0.0).astype(jnp.bfloat16)
 
 
 def eliminate(matrix):
@@ -221,21 +227,23 @@
         if h == 0:
             pl.semaphore_wait(barrier, cols - 1 + PLANE)
         copies.append(send(s_src.at[h], s_dst.at[h], pair_sem, h, (1 - me_r, me_c)))
-    total = jnp.zeros((row_blocks * width, order), jnp.float32)
+    total = jnp.zeros((order, row_blocks * width), jnp.float32)
     for h in range(halves):
         part = slice(h * half, (h + 1) * half)
         copies[h].wait_recv()
         summed = mine[h] + s_dst[h].astype(jnp.float32)
         for j in range(col_blocks):
             scaled = strip(theta_ref, j)[:, part] * summed[j * width : (j + 1) * width]
-            zs[h, j] = scaled.astype(jnp.bfloat16).astype(jnp.float32)
+            scaled = scaled.astype(jnp.bfloat16).astype(jnp.float32)
+            zs[h, j] = jnp.concatenate([scaled] * row_blocks, axis=0).T
         for n in range(stored):
-            left = spread(zs.at[h], bcol_ref[n], brow_ref[n], row_blocks, row_blocks * width)
-            total = total + dot_nt(left, vals[n, :, part])
-    for i in range(row_blocks):
-        for p in range(pieces):
+            right = spread_lanes(zs.at[h], bcol_ref[n], brow_ref[n], width)
+            total = total + jnp.dot(vals[n, :, part], right, preferred_element_type=jnp.float32)
+    for p in range(pieces):
+        turned = total[p * LANES : (p + 1) * LANES].T
+        for i in range(row_blocks):
             at = pieces * i + p
-            y_own[at % 2, at // 2] = total[i * width : (i + 1) * width, p * LANES : (p + 1) * LANES]
+            y_own[at % 2, at // 2] = turned[i * width : (i + 1) * width]
     copy = send(y_own.at[1 - core], y_pair, pair_sem, halves, twin)
     copy.wait_recv()
     for t in range(chips):
@@ -297,18 +305,19 @@
     image_cols = e_src[...] + e_dst[...]
     for j in range(col_blocks):
         line = (strip(theta_ref, j) * image_cols[j : j + 1]).astype(jnp.bfloat16)
-        zv[j] = line.astype(jnp.float32)
-    total = jnp.zeros((16, order), jnp.float32)
+        zv[j] = jnp.broadcast_to(line.astype(jnp.float32), (LANES, order)).T
+    total = jnp.zeros((order, LANES), jnp.float32)
     for n in range(stored):
-        left = spread(zv, bcol_ref[n], brow_ref[n], row_blocks, 16)
-        total = total + dot_nt(left, vals[n])
+        right = spread_lanes(zv, bcol_ref[n], brow_ref[n], width)
+        total = total + jnp.dot(vals[n], right, preferred_element_type=jnp.float32)
+    turned = [total[p * LANES : (p + 1) * LANES].T for p in range(pieces)]
 
     against = regularize * y_t * direction
     curvature = regularize * direction * direction
     for i in range(row_blocks):
         for p in range(pieces):
             part = slice(p * LANES, (p + 1) * LANES)
-            piece = total[i : i + 1, part]
+            piece = turned[p][i * width : i * width + 1]
             f_src[pieces * i + p, 0:1] = piece
             against = against + y_all[(pieces * i + p) % 2, (pieces * i + p) // 2] * piece
             curvature = curvature + lines[i][:, part] * piece
@@ -371,7 +380,7 @@
             pltpu.VMEM((row_blocks, width, order), f32),
             pltpu.VMEM((2, col_blocks * width, order // 2), bf16),
             pltpu.VMEM((2, col_blocks * width, order // 2), bf16),
-            pltpu.VMEM((2, col_blocks, width, order // 2), f32),
+            pltpu.VMEM((2, col_blocks, order // 2, row_blocks * width), f32),
             pltpu.VMEM((2, cols // 2, width, LANES), f32),
             pltpu.VMEM((cols // 2, width, LANES), f32),
             pltpu.VMEM((cols // 2, width, LANES), f32),
@@ -382,7 +391,7 @@
             pltpu.VMEM((row_blocks, 1, order), f32),
             pltpu.VMEM((8, order), f32),
             pltpu.VMEM((8, order), f32),
-            pltpu.VMEM((col_blocks, 1, order), f32),
+            pltpu.VMEM((col_blocks, order, LANES), f32),
             pltpu.VMEM((cols, 2, LANES), f32),
             pltpu.VMEM((cols, 2, LANES), f32),
             pltpu.VMEM((2, LANES), f32),

time: 42.2 us -> 42.7 us (1.012)
  no operation moved by 1% of the time
where the time goes in v4:
time: 42.7 us; the launch traced here: 42.5 us
  Pallas kernels  40.5 us (95%)
  other arithmetic  1.38 us (3%)
  between operations  0.64 us (1%)
    pallas_call x1, Pallas kernels, fused(): pl.pallas_call(functools.partial(kernel, cols, row_blocks, col_blocks), o...  40.5 us
    sub x1, other arithmetic, fused(): return (iterate, residual, (residual - taken) / precond_shift)  1.38 us

profile of v4, /device:TPU:0, one launch (start us, length us, event | category | flops | bytes accessed | tf_op | source)
XLA Modules:
  0.0 42.5 jit_solution(4106781282449965081)
XLA Ops:
  0.6 40.5 %shard_map.85 = f32[8,128]{1,0:T(8,128)} custom-call(s32[8]{0:T(128)} %bitcast.18, s32[8]{0:T(128)} %bitcast.19, bf16[8,512,512]{2,1,0:T(8,128)(2,1)} %bitcast.14, bf16[32,2048]{1,0:T(8,128)(2,1)} %bitcast.15, f32[16,128]{1,0:T(8,128)} %bitcast.16, f32[16,128]{1,0:T(8,128)} %bitcast.17), custom_call_target="tpu_custom_call" | custom-call | tf_op jit(solution)/shard_map/pallas_call | solution.py:368
  41.1 1.4 %bitcast_subtract_fusion = (f32[128]{0:T(128)}, f32[128]{0:T(128)}, f32[128]{0:T(128)}) fusion(f32[8,128]{1,0:T(8,128)} %shard_map.85), kind=kLoop, calls=%fused_computation | loop fusion | flops 768 | bytes 4096 | tf_op jit(solution)/shard_map/sub | solution.py:420

commit v5 on v3

--- a/solution.py
+++ b/solution.py
@@ -100,6 +100,7 @@
     a_sem,
     g_sem,
     f_sem,
+    h_sem,
 ):
     me_r = lax.axis_index("row")
     me_c = lax.axis_index("col")
@@ -138,9 +139,9 @@
         pl.semaphore_signal(
             barrier, inc=1, device_id=(me_r, lax.rem(me_c + t, cols)), device_id_type=MESH
         )
-    for u in range(PLANE):
+    for t in range(cols):
         pl.semaphore_signal(
-            barrier, inc=1, device_id=(1 - me_r, z * PLANE + u), device_id_type=MESH
+            barrier, inc=1, device_id=(1 - me_r, lax.rem(me_c + t, cols)), device_id_type=MESH
         )
 
     def send(src, dst, sems, at, device):
@@ -208,7 +209,7 @@
     lefts = [
         spread(sk_t, brow_ref[n], bcol_ref[n], col_blocks, col_blocks * width) for n in range(stored)
     ]
-    mine, copies = [], []
+    copies = []
     for h in range(halves):
         part = slice(h * half, (h + 1) * half)
         total = jnp.zeros((col_blocks * width, half), jnp.float32)
@@ -216,16 +217,15 @@
             if h == 0:
                 loads[n].wait()
             total = total + jnp.dot(lefts[n], vals[n, :, part], preferred_element_type=jnp.float32)
-        s_src[h] = total.astype(jnp.bfloat16)
-        mine.append(total)
+        s_src[h] = total
         if h == 0:
-            pl.semaphore_wait(barrier, cols - 1 + PLANE)
+            pl.semaphore_wait(barrier, 2 * cols - 1)
         copies.append(send(s_src.at[h], s_dst.at[h], pair_sem, h, (1 - me_r, me_c)))
     total = jnp.zeros((row_blocks * width, order), jnp.float32)
     for h in range(halves):
         part = slice(h * half, (h + 1) * half)
         copies[h].wait_recv()
-        summed = mine[h] + s_dst[h].astype(jnp.float32)
+        summed = s_src[h] + s_dst[h]
         for j in range(col_blocks):
             scaled = strip(theta_ref, j)[:, part] * summed[j * width : (j + 1) * width]
             zs[h, j] = scaled.astype(jnp.bfloat16).astype(jnp.float32)
@@ -320,18 +320,23 @@
     along = jnp.sum(rhs[:1] * direction, axis=1, keepdims=True)
     lane = lax.broadcasted_iota(jnp.int32, (1, LANES), 1)
     value = jnp.where(lane == width, curvature, jnp.where(lane == width + 1, along, against))
+    h_src[...] = value
     for to in range(cols):
         f_src[to, 1:2] = value
     copies = []
     for t in range(1, cols):
         to = lax.rem(me_c + t, cols)
         copies.append(send(f_src.at[to], f_dst.at[t], f_sem, t, (me_r, to)))
+    crossed = []
+    for t in range(cols):
+        to = lax.rem(me_c + t, cols)
+        crossed.append(send(h_src, h_dst.at[t], h_sem, t, (1 - me_r, to)))
     gathered = scatter_finish(f_src[me_c], copies, f_dst)
-    h_src[...] = gathered
-    copy = send(h_src, h_dst, pair_sem, halves + 2, (1 - me_r, me_c))
     image = gathered[0:1]
-    copy.wait_recv()
-    summed = gathered[1:2] + h_dst[1:2]
+    summed = gathered[1:2]
+    for t, copy in enumerate(crossed):
+        copy.wait_recv()
+        summed = summed + h_dst[t]
     alpha = summed[:, width + 1 : width + 2] / summed[:, width : width + 1]
     sketched = jnp.sum(jnp.where(diagonal, summed, 0.0), axis=1, keepdims=True)
     taken = jnp.sum((sketched_rhs - alpha * sketched) * weights, axis=0, keepdims=True)
@@ -369,8 +374,8 @@
             pltpu.VMEM((local // LANES, LANES), f32),
             pltpu.VMEM((stored, order, order), bf16),
             pltpu.VMEM((row_blocks, width, order), f32),
-            pltpu.VMEM((2, col_blocks * width, order // 2), bf16),
-            pltpu.VMEM((2, col_blocks * width, order // 2), bf16),
+            pltpu.VMEM((2, col_blocks * width, order // 2), f32),
+            pltpu.VMEM((2, col_blocks * width, order // 2), f32),
             pltpu.VMEM((2, col_blocks, width, order // 2), f32),
             pltpu.VMEM((2, cols // 2, width, LANES), f32),
             pltpu.VMEM((cols // 2, width, LANES), f32),
@@ -385,13 +390,14 @@
             pltpu.VMEM((col_blocks, 1, order), f32),
             pltpu.VMEM((cols, 2, LANES), f32),
             pltpu.VMEM((cols, 2, LANES), f32),
-            pltpu.VMEM((2, LANES), f32),
-            pltpu.VMEM((2, LANES), f32),
+            pltpu.VMEM((1, LANES), f32),
+            pltpu.VMEM((cols, 1, LANES), f32),
             pltpu.SemaphoreType.DMA((stored + 5,)),
-            pltpu.SemaphoreType.DMA((2, 5)),
+            pltpu.SemaphoreType.DMA((2, 4)),
             col_sems,
             col_sems,
             reduce_sems,
+            col_sems,
             col_sems,
         ],
         compiler_params=pltpu.CompilerParams(

time: 42.2 us -> 43.9 us (1.040)
  Pallas kernels: 40.1 us -> 41.8 us
    pallas_call x1, Pallas kernels: 40.1 us -> 41.8 us  [fused(): pl.pallas_call(functools.partial(kernel, cols, row_blocks, col_blocks), o...]
where the time goes in v5:
time: 43.9 us; the launch traced here: 43.8 us
  Pallas kernels  41.8 us (95%)
  other arithmetic  1.38 us (3%)
  between operations  0.64 us (1%)
    pallas_call x1, Pallas kernels, fused(): pl.pallas_call(functools.partial(kernel, cols, row_blocks, col_blocks), o...  41.8 us
    sub x1, other arithmetic, fused(): return (iterate, residual, (residual - taken) / precond_shift)  1.38 us

profile of v5, /device:TPU:0, one launch (start us, length us, event | category | flops | bytes accessed | tf_op | source)
XLA Modules:
  0.0 43.8 jit_solution(7379936681586010622)
XLA Ops:
  0.6 41.8 %shard_map.85 = f32[8,128]{1,0:T(8,128)} custom-call(s32[8]{0:T(128)} %bitcast.18, s32[8]{0:T(128)} %bitcast.19, bf16[8,512,512]{2,1,0:T(8,128)(2,1)} %bitcast.14, bf16[32,2048]{1,0:T(8,128)(2,1)} %bitcast.15, f32[16,128]{1,0:T(8,128)} %bitcast.16, f32[16,128]{1,0:T(8,128)} %bitcast.17), custom_call_target="tpu_custom_call" | custom-call | tf_op jit(solution)/shard_map/pallas_call | solution.py:364
  42.4 1.4 %bitcast_subtract_fusion = (f32[128]{0:T(128)}, f32[128]{0:T(128)}, f32[128]{0:T(128)}) fusion(f32[8,128]{1,0:T(8,128)} %shard_map.85), kind=kLoop, calls=%fused_computation | loop fusion | flops 768 | bytes 4096 | tf_op jit(solution)/shard_map/sub | solution.py:417

commit v6 on v5

--- a/solution.py
+++ b/solution.py
@@ -45,16 +45,24 @@
         columns = [
             jnp.broadcast_to(wide[:, k : k + 1], (order, LANES)) for k in range(start, start + panel)
         ]
-        for j in range(panel):
+        for j in range(0, panel, 2):
             k = start + j
-            here = at == k
-            column = columns[j]
-            inverse = 1.0 / column[k : k + 1]
-            for other in range(j + 1, panel):
-                row = columns[other][k : k + 1] * inverse
-                columns[other] = jnp.where(here, row, columns[other] - column * row)
-            row = wide[k : k + 1] * inverse
-            wide = jnp.where(here, row, wide - column * row)
+            left, right = columns[j], columns[j + 1]
+            first = 1.0 / left[k : k + 1]
+            ratio = right[k : k + 1] * first
+            below = left[k + 1 : k + 2]
+            second = 1.0 / (right[k + 1 : k + 2] - below * ratio)
+
+            def clear(target):
+                upper = target[k : k + 1] * first
+                lower = (target[k + 1 : k + 2] - below * upper) * second
+                upper = upper - ratio * lower
+                rest = target - left * upper - right * lower
+                return jnp.where(at == k, upper, jnp.where(at == k + 1, lower, rest))
+
+            for other in range(j + 2, panel):
+                columns[other] = clear(columns[other])
+            wide = clear(wide)
     return wide[:, order : order + 1], wide[:, 2 * order : 3 * order]
 
 

time: 43.9 us -> 44 us (level)
  no operation moved by 1% of the time
where the time goes in v6:
time: 44 us; the launch traced here: 43.9 us
  Pallas kernels  41.9 us (95%)
  other arithmetic  1.38 us (3%)
  between operations  0.64 us (1%)
    pallas_call x1, Pallas kernels, fused(): pl.pallas_call(functools.partial(kernel, cols, row_blocks, col_blocks), o...  41.9 us
    sub x1, other arithmetic, fused(): return (iterate, residual, (residual - taken) / precond_shift)  1.38 us

profile of v6, /device:TPU:0, one launch (start us, length us, event | category | flops | bytes accessed | tf_op | source)
XLA Modules:
  0.0 43.9 jit_solution(6757348089705824643)
XLA Ops:
  0.6 41.9 %shard_map.85 = f32[8,128]{1,0:T(8,128)} custom-call(s32[8]{0:T(128)} %bitcast.18, s32[8]{0:T(128)} %bitcast.19, bf16[8,512,512]{2,1,0:T(8,128)(2,1)} %bitcast.14, bf16[32,2048]{1,0:T(8,128)(2,1)} %bitcast.15, f32[16,128]{1,0:T(8,128)} %bitcast.16, f32[16,128]{1,0:T(8,128)} %bitcast.17), custom_call_target="tpu_custom_call" | custom-call | tf_op jit(solution)/shard_map/pallas_call | solution.py:372
  42.5 1.4 %bitcast_subtract_fusion = (f32[128]{0:T(128)}, f32[128]{0:T(128)}, f32[128]{0:T(128)}) fusion(f32[8,128]{1,0:T(8,128)} %shard_map.85), kind=kLoop, calls=%fused_computation | loop fusion | flops 768 | bytes 4096 | tf_op jit(solution)/shard_map/sub | solution.py:425
